TPU v7x, 128 devices: a whole 4x4x4 slice. The times are simulated.
128 devices in a mesh: section: 8 (over z, y_lo), shard: 16 (over y_hi, x, core).
Axes of the slice: x: 4, y: 4 (y_hi: 2, y_lo: 2; y = y_hi * 2 + y_lo), z: 4, core: 2. Of those that a mesh axis runs over, the one named last changes fastest.
Arguments:
- saved_inputs: bfloat16 [8, 8192, 2048], P('section', 'shard'), may hold values from -6 to 6
- grad_out: bfloat16 [8192, 2048], P('shard'), may hold values from -6 to 6
- w_in: bfloat16 [8, 2048, 4096], P('section', 'shard'), may hold values from -0.125 to 0.125
- w_out: bfloat16 [8, 4096, 2048], P('section', 'shard'), may hold values from -0.09375 to 0.09375
- skip_gain: float32 [4, 2048], replicated, may hold values from 0.5 to 1.5
- proj_model: bfloat16 [8, 2048, 128], P('section'), may hold values from -0.125 to 0.125
- proj_hidden: bfloat16 [8, 4096, 128], P('section'), may hold values from -0.09375 to 0.09375
Outputs:
- features: float32 [32, 4096], P('shard', 'section')
All inputs are finite; a program needn't handle non-finite values.
Results may differ from a plain program's by a relative error of at most 0.02.
Values may be sent and summed in bfloat16 or wider, within the bound.
A program may use at most 128 MiB of HBM per device.

v0:
```python
import math

import jax
import jax.numpy as jnp
from jax import lax
from jax.sharding import PartitionSpec as P

SEQ = 256


square_root_half = 1.0 / math.sqrt(2.0)
inv_root_two_pi = 1.0 / math.sqrt(2.0 * math.pi)


def partner(value, axis, bit):
    return lax.ppermute(value, axis, [(i, i ^ 1 << bit) for i in range(lax.axis_size(axis))])


def from_behind(value, axis, by):
    length = lax.axis_size(axis)
    pairs = [(i, i + by) for i in range(length) if 0 <= i + by < length]
    return lax.ppermute(value, axis, pairs)


def gelu_parts(value):
    cumulative = 0.5 * (1.0 + jax.scipy.special.erf(value * square_root_half))
    density = jnp.exp(-0.5 * value * value) * inv_root_two_pi
    return (value * cumulative, cumulative + value * density)


def mirror_index(value, sections):
    for bit in range(sections.bit_length() - 1):
        value = partner(value, "section", bit)
    return value


def place(buffer, value, slot, valid):
    old = lax.dynamic_index_in_dim(buffer, slot, 0, keepdims=False)
    return lax.dynamic_update_index_in_dim(buffer, jnp.where(valid, value, old), slot, 0)


def body(saved_inputs, grad_out, w_in, w_out, skip_gain, proj_model, proj_hidden):
    sections = lax.axis_size("section")
    half = sections // 2
    section = lax.axis_index("section")
    gathered_in, gathered_out = (
        lax.all_gather(w_in, "shard", axis=1, tiled=True),
        lax.all_gather(w_out, "shard", axis=1, tiled=True),
    )
    w_first = gathered_in[0]
    w_second = gathered_out[0]
    inputs = saved_inputs[0]
    model_proj = proj_model[0]
    hidden_proj = proj_hidden[0]
    tok_dev, width = inputs.shape
    proj_width = model_proj.shape[1] // 2
    pieces = 4
    delay = pieces - 1
    piece_rows = tok_dev // pieces
    group_rows = min(piece_rows, SEQ)
    groups = piece_rows // group_rows
    sample_count = tok_dev // SEQ
    gain_row = lax.dynamic_index_in_dim(
        skip_gain, jnp.clip(section - half, 0, half - 1), 0, keepdims=False
    )
    is_top = section == sections - 1
    is_encoder = section < half
    start_tick = sections - 1 - section + jnp.where(is_encoder, delay, 0)
    sender_start = sections - 2 - section + jnp.where(section + 1 < half, delay, 0)
    scale = SEQ ** (-0.5)

    def compute(grad, slot):
        rows = lax.dynamic_slice_in_dim(inputs, slot * piece_rows, piece_rows, 0)
        pre_act = jnp.dot(rows, w_first, preferred_element_type=jnp.float32)
        act, slope = gelu_parts(pre_act)
        hidden = act.astype(jnp.bfloat16)
        grad_hidden = lax.dot_general(
            grad, w_second, (((1,), (1,)), ((), ())), preferred_element_type=jnp.float32
        )
        grad_pre = (grad_hidden * slope).astype(jnp.bfloat16)
        grad_x = grad.astype(jnp.float32) + lax.dot_general(
            grad_pre, w_first, (((1,), (1,)), ((), ())), preferred_element_type=jnp.float32
        )
        in_first = jnp.dot(rows, model_proj[:, :proj_width], preferred_element_type=jnp.float32)
        out_first = jnp.dot(
            grad_pre, hidden_proj[:, :proj_width], preferred_element_type=jnp.float32
        )
        in_second = jnp.dot(hidden, hidden_proj[:, proj_width:], preferred_element_type=jnp.float32)
        out_second = jnp.dot(grad, model_proj[:, proj_width:], preferred_element_type=jnp.float32)
        shape = (groups, group_rows, proj_width)
        term = jnp.einsum(
            "anf,anj->afj",
            in_first.reshape(shape),
            out_first.reshape(shape),
            precision=lax.Precision.HIGHEST,
        )
        term = term + jnp.einsum(
            "anf,anj->afj",
            in_second.reshape(shape),
            out_second.reshape(shape),
            precision=lax.Precision.HIGHEST,
        )
        return (
            grad_x.astype(jnp.bfloat16),
            (grad_x * gain_row[None, :]).astype(jnp.bfloat16),
            term,
        )

    def resting(grad, slot):
        empty = jnp.zeros((piece_rows, width), jnp.bfloat16)
        return (empty, empty, jnp.zeros((groups, proj_width, proj_width), jnp.float32))

    def tick(step, state):
        inbox, skipbox, skip_out, totals = state
        current = step - start_tick
        is_working = (current >= 0) & (current < pieces)
        slot = jnp.clip(current, 0, pieces - 1)
        from_above = lax.dynamic_index_in_dim(inbox, slot, 0, keepdims=False)
        skip_in = lax.dynamic_index_in_dim(skipbox, slot, 0, keepdims=False)
        top_rows = lax.dynamic_slice_in_dim(grad_out, slot * piece_rows, piece_rows, 0)
        summed = (from_above.astype(jnp.float32) + skip_in.astype(jnp.float32)).astype(jnp.bfloat16)
        grad = jnp.where(is_top, top_rows, jnp.where(is_encoder, summed, from_above))
        sent, skip_value, term = lax.cond(is_working, compute, resting, grad, slot)
        first = slot * piece_rows // SEQ
        part = lax.dynamic_slice_in_dim(totals, first, groups, 0)
        totals = lax.dynamic_update_slice_in_dim(totals, part + term, first, 0)
        skip_out = place(skip_out, skip_value, slot, is_working & jnp.logical_not(is_encoder))
        received = from_behind(sent, "section", -1)
        arrived = step - sender_start
        fresh = (arrived >= 0) & (arrived < pieces) & (section < sections - 1)
        inbox = place(inbox, received, jnp.clip(arrived, 0, pieces - 1), fresh)
        return (inbox, skipbox, skip_out, totals)

    buffer = jnp.zeros((pieces, piece_rows, width), jnp.bfloat16)
    state = (buffer, buffer, buffer, jnp.zeros((sample_count, proj_width, proj_width), jnp.float32))
    last_tick = sections + pieces - 1 + delay
    middle = half + pieces - 1
    state = lax.fori_loop(0, middle, tick, state)
    inbox, skipbox, skip_out, totals = state
    skipbox = mirror_index(skip_out, sections)
    state = lax.fori_loop(middle, last_tick, tick, (inbox, skipbox, skip_out, totals))
    totals = state[3]
    flat = totals.reshape(sample_count, proj_width * proj_width) * scale
    return lax.psum_scatter(flat, "section", scatter_dimension=1, tiled=True)


def solution(mesh):
    placed = (
        P("section", "shard", None),
        P("shard", None),
        P("section", "shard", None),
        P("section", "shard", None),
        P(),
        P("section", None, None),
        P("section", None, None),
    )
    return jax.shard_map(
        body, mesh=mesh, in_specs=placed, out_specs=P("shard", "section"), check_vma=False
    )
```

profile of v0, /device:TPU:1, one launch (start us, length us, event | category | flops | bytes accessed | tf_op | source)
XLA Modules:
  0.0 1231.3 jit_solution(4089708889121777279)
XLA Ops:
  8.1 115.6 %all-gather.3.cloned.1.call-done = bf16[1,4096,2048]{2,1,0:T(8,128)(2,1)} async-done(((bf16[1,256,2048]{2,1,0:T(8,128)(2,1)}), bf16[1,4096,2048]{2,1,0:T(8,128)(2,1)}) %all-gather.3.cloned.1.call-update) | async-done | bytes 16777232 | tf_op jit(solution)/shard_map/all_gather | solution.py:48
  123.7 110.5 %all-gather.5.cloned.1.call-done = bf16[1,2048,4096]{2,1,0:T(8,128)(2,1)} async-done(((bf16[1,128,4096]{2,1,0:T(8,128)(2,1)}), bf16[1,2048,4096]{2,1,0:T(8,128)(2,1)}) %all-gather.5.cloned.1.call-update) | async-done | bytes 16777232 | tf_op jit(solution)/shard_map/all_gather | solution.py:47
  236.1 273.0 %while.37 = (s32[]{:T(128)}, bf16[4,128,2048]{2,1,0:T(8,128)(2,1)S(1)}, bf16[4,128,2048]{2,1,0:T(8,128)(2,1)}, f32[2,64,64]{2,1,0:T(8,128)S(1)}, s32[]{:T(128)},...) while((s32[]{:T(128)}, ...), condition=%wide.region_3.4_spmd, body=%wide.region_0.3_spmd.sunk | while | flops 6666330112 | bytes 88499552 | solution.py:138
  335.4 173.3 %collective-permute-done = bf16[128,2048]{1,0:T(8,128)(2,1)} collective-permute-done((bf16[128,2048]{1,0:T(8,128)(2,1)}, bf16[128,2048]{1,0:T(8,128)(2,1)}, u32[]{:S(2)}, u32[]{:S(2)}) %collective-permute-start) | collective-permute-done | bytes 524320 | tf_op jit(solution)/shard_map/while/body/eval_jaxpr/ppermute | solution.py:22
  509.1 42.4 %collective-permute-start.2 = (bf16[4,128,2048]{2,1,0:T(8,128)(2,1)}, bf16[4,128,2048]{2,1,0:T(8,128)(2,1)S(1)}, u32[]{:S(2)}, u32[]{:S(2)}) collective-permute-start(bf16[4,128,2048]{2,1,0:T(8,128)(2,1)} %get-tuple-element.1061), channel_id=1, source_target_pairs={{0,16},{16,0},{32,48},{48,32},{64,80},{80,64},{96,112},{112,96},{1... | collective-permute-start | bytes 6291464 | tf_op jit(solution)/shard_map/ppermute | solution.py:16
  551.4 41.4 %collective-permute-done.2 = bf16[4,128,2048]{2,1,0:T(8,128)(2,1)S(1)} collective-permute-done((bf16[4,128,2048]{2,1,0:T(8,128)(2,1)}, bf16[4,128,2048]{2,1,0:T(8,128)(2,1)S(1)}, u32[]{:S(2)}, u32[]{:S(2)}) %collective-permute-start.2) | collective-permute-done | bytes 2097184 | tf_op jit(solution)/shard_map/ppermute | solution.py:16
  592.8 81.9 %collective-permute-start.3 = (bf16[4,128,2048]{2,1,0:T(8,128)(2,1)S(1)}, bf16[4,128,2048]{2,1,0:T(8,128)(2,1)}, u32[]{:S(2)}, u32[]{:S(2)}) collective-permute-start(bf16[4,128,2048]{2,1,0:T(8,128)(2,1)S(1)} %collective-permute-done.2), channel_id=1, source_target_pairs={{0,32},{16,48},{32,0},{48,16},{64,96},{80,112},{96,64},{112,80},{1... | collective-permute-start | bytes 6291464 | tf_op jit(solution)/shard_map/ppermute | solution.py:16
  674.7 38.3 %collective-permute-done.3 = bf16[4,128,2048]{2,1,0:T(8,128)(2,1)} collective-permute-done((bf16[4,128,2048]{2,1,0:T(8,128)(2,1)S(1)}, bf16[4,128,2048]{2,1,0:T(8,128)(2,1)}, u32[]{:S(2)}, u32[]{:S(2)}) %collective-permute-start.3) | collective-permute-done | bytes 2097184 | tf_op jit(solution)/shard_map/ppermute | solution.py:16
  719.2 41.7 %collective-permute-done.4 = bf16[4,128,2048]{2,1,0:T(8,128)(2,1)} collective-permute-done((bf16[4,128,2048]{2,1,0:T(8,128)(2,1)}, bf16[4,128,2048]{2,1,0:T(8,128)(2,1)}, u32[]{:S(2)}, u32[]{:S(2)}) %collective-permute-start.4) | collective-permute-done | bytes 2097184 | tf_op jit(solution)/shard_map/ppermute | solution.py:16
  760.9 398.5 %while.38 = (s32[]{:T(128)}, bf16[4,128,2048]{2,1,0:T(8,128)(2,1)S(1)}, f32[2,64,64]{2,1,0:T(8,128)S(1)}, s32[]{:T(128)}, pred[]{:T(512)}, /*index=5*/s32[]{:T(1...) while((s32[]{:T(128)}, ...), condition=%wide.region_7.8_spmd, body=%wide.region_4.7_spmd.sunk | while | flops 6666854400 | bytes 88490848 | solution.py:141
  798.1 131.5 %collective-permute-done.1 = bf16[128,2048]{1,0:T(8,128)(2,1)S(1)} collective-permute-done((bf16[128,2048]{1,0:T(8,128)(2,1)}, bf16[128,2048]{1,0:T(8,128)(2,1)S(1)}, u32[]{:S(2)}, u32[]{:S(2)}) %collective-permute-start.1) | collective-permute-done | bytes 524320 | tf_op jit(solution)/shard_map/while/body/eval_jaxpr/ppermute | solution.py:22
  933.9 42.1 %conditional.5 = (bf16[128,2048]{1,0:T(8,128)(2,1)}, f32[1,64,64]{2,1,0:T(8,128)S(1)}) conditional(s32[]{:T(128)} %convert_element_type.149, () %tuple.121, (pred[]{:T(512)}, s32[]{:T(128)}, pred[]{:T(512)}, bf16[512,2048]{1,0:T(8,128)(2,1)}, pred[]{:T(512)}, /*index=5*/bf16[128,2048]{1,0:T(8,128)(2,1)}, bf16[128,2048]{1,0:T(8,128)(2,1)}, ...), branch_computations={%region_5.5_spmd, %region_6.6_spmd} | conditional | flops 6665539584 | bytes 81051800 | solution.py:123
  945.1 13.1 %fusion.19 = bf16[128,4096]{1,0:T(8,128)(2,1)} fusion(bf16[128,2048]{1,0:T(8,128)(2,1)S(1)} %select_select_fusion, bf16[4096,2048]{1,0:T(8,128)(2,1)} %get-tuple-element.1031, f32[128,4096]{1,0:T(8,128)} %fusion.35), kind=kOutput, calls=%fused_computation.35 | convolution fusion | flops 2152726528 | bytes 20447232 | tf_op jit(solution)/shard_map/while/body/eval_jaxpr/cond/branch_1_fun/dot_general | solution.py:77
  963.4 12.6 %fusion.20 = bf16[128,2048]{1,0:T(8,128)(2,1)} fusion(bf16[128,4096]{1,0:T(8,128)(2,1)} %fusion.19, bf16[2048,4096]{1,0:T(8,128)(2,1)} %get-tuple-element.1034, bf16[128,2048]{1,0:T(8,128)(2,1)S(1)} %select_select_fusion), kind=kOutput, calls=%fused_computation.38 | convolution fusion | flops 2148270080 | bytes 18874368 | tf_op jit(solution)/shard_map/while/body/eval_jaxpr/cond/branch_1_fun/dot_general | solution.py:81
  991.3 42.1 %conditional.5 = (bf16[128,2048]{1,0:T(8,128)(2,1)}, f32[1,64,64]{2,1,0:T(8,128)S(1)}) conditional(s32[]{:T(128)} %convert_element_type.149, () %tuple.121, (pred[]{:T(512)}, s32[]{:T(128)}, pred[]{:T(512)}, bf16[512,2048]{1,0:T(8,128)(2,1)}, pred[]{:T(512)}, /*index=5*/bf16[128,2048]{1,0:T(8,128)(2,1)}, bf16[128,2048]{1,0:T(8,128)(2,1)}, ...), branch_computations={%region_5.5_spmd, %region_6.6_spmd} | conditional | flops 6665539584 | bytes 81051800 | solution.py:123
  1002.5 13.1 %fusion.19 = bf16[128,4096]{1,0:T(8,128)(2,1)} fusion(bf16[128,2048]{1,0:T(8,128)(2,1)S(1)} %select_select_fusion, bf16[4096,2048]{1,0:T(8,128)(2,1)} %get-tuple-element.1031, f32[128,4096]{1,0:T(8,128)} %fusion.35), kind=kOutput, calls=%fused_computation.35 | convolution fusion | flops 2152726528 | bytes 20447232 | tf_op jit(solution)/shard_map/while/body/eval_jaxpr/cond/branch_1_fun/dot_general | solution.py:77
  1020.8 12.6 %fusion.20 = bf16[128,2048]{1,0:T(8,128)(2,1)} fusion(bf16[128,4096]{1,0:T(8,128)(2,1)} %fusion.19, bf16[2048,4096]{1,0:T(8,128)(2,1)} %get-tuple-element.1034, bf16[128,2048]{1,0:T(8,128)(2,1)S(1)} %select_select_fusion), kind=kOutput, calls=%fused_computation.38 | convolution fusion | flops 2148270080 | bytes 18874368 | tf_op jit(solution)/shard_map/while/body/eval_jaxpr/cond/branch_1_fun/dot_general | solution.py:81
  1048.7 42.1 %conditional.5 = (bf16[128,2048]{1,0:T(8,128)(2,1)}, f32[1,64,64]{2,1,0:T(8,128)S(1)}) conditional(s32[]{:T(128)} %convert_element_type.149, () %tuple.121, (pred[]{:T(512)}, s32[]{:T(128)}, pred[]{:T(512)}, bf16[512,2048]{1,0:T(8,128)(2,1)}, pred[]{:T(512)}, /*index=5*/bf16[128,2048]{1,0:T(8,128)(2,1)}, bf16[128,2048]{1,0:T(8,128)(2,1)}, ...), branch_computations={%region_5.5_spmd, %region_6.6_spmd} | conditional | flops 6665539584 | bytes 81051800 | solution.py:123
  1059.8 13.1 %fusion.19 = bf16[128,4096]{1,0:T(8,128)(2,1)} fusion(bf16[128,2048]{1,0:T(8,128)(2,1)S(1)} %select_select_fusion, bf16[4096,2048]{1,0:T(8,128)(2,1)} %get-tuple-element.1031, f32[128,4096]{1,0:T(8,128)} %fusion.35), kind=kOutput, calls=%fused_computation.35 | convolution fusion | flops 2152726528 | bytes 20447232 | tf_op jit(solution)/shard_map/while/body/eval_jaxpr/cond/branch_1_fun/dot_general | solution.py:77
  1078.2 12.6 %fusion.20 = bf16[128,2048]{1,0:T(8,128)(2,1)} fusion(bf16[128,4096]{1,0:T(8,128)(2,1)} %fusion.19, bf16[2048,4096]{1,0:T(8,128)(2,1)} %get-tuple-element.1034, bf16[128,2048]{1,0:T(8,128)(2,1)S(1)} %select_select_fusion), kind=kOutput, calls=%fused_computation.38 | convolution fusion | flops 2148270080 | bytes 18874368 | tf_op jit(solution)/shard_map/while/body/eval_jaxpr/cond/branch_1_fun/dot_general | solution.py:81
  1106.0 42.1 %conditional.5 = (bf16[128,2048]{1,0:T(8,128)(2,1)}, f32[1,64,64]{2,1,0:T(8,128)S(1)}) conditional(s32[]{:T(128)} %convert_element_type.149, () %tuple.121, (pred[]{:T(512)}, s32[]{:T(128)}, pred[]{:T(512)}, bf16[512,2048]{1,0:T(8,128)(2,1)}, pred[]{:T(512)}, /*index=5*/bf16[128,2048]{1,0:T(8,128)(2,1)}, bf16[128,2048]{1,0:T(8,128)(2,1)}, ...), branch_computations={%region_5.5_spmd, %region_6.6_spmd} | conditional | flops 6665539584 | bytes 81051800 | solution.py:123
  1117.2 13.1 %fusion.19 = bf16[128,4096]{1,0:T(8,128)(2,1)} fusion(bf16[128,2048]{1,0:T(8,128)(2,1)S(1)} %select_select_fusion, bf16[4096,2048]{1,0:T(8,128)(2,1)} %get-tuple-element.1031, f32[128,4096]{1,0:T(8,128)} %fusion.35), kind=kOutput, calls=%fused_computation.35 | convolution fusion | flops 2152726528 | bytes 20447232 | tf_op jit(solution)/shard_map/while/body/eval_jaxpr/cond/branch_1_fun/dot_general | solution.py:77
  1135.5 12.6 %fusion.20 = bf16[128,2048]{1,0:T(8,128)(2,1)} fusion(bf16[128,4096]{1,0:T(8,128)(2,1)} %fusion.19, bf16[2048,4096]{1,0:T(8,128)(2,1)} %get-tuple-element.1034, bf16[128,2048]{1,0:T(8,128)(2,1)S(1)} %select_select_fusion), kind=kOutput, calls=%fused_computation.38 | convolution fusion | flops 2148270080 | bytes 18874368 | tf_op jit(solution)/shard_map/while/body/eval_jaxpr/cond/branch_1_fun/dot_general | solution.py:81
  1161.5 61.6 %reduce-scatter.4.cloned.1.call-done = f32[512,2]{1,0:T(8,128)} async-done(((f32[4096,2]{1,0:T(8,128)}), f32[512,2]{1,0:T(8,128)}) %reduce-scatter.4.cloned.1.call-update) | async-done | bytes 4112
  (187 shorter events, 290.1 us)
Async XLA Ops:
  6.5 117.1 %all-gather.3.cloned.1.call-start = ((), (), s32[]{:S(2)}) async-start(), calls=%async_computation.1 | async-start | bytes 17825792 | tf_op jit(solution)/shard_map/all_gather | solution.py:48
  7.3 226.9 %all-gather.5.cloned.1.call-start = ((), (), s32[]{:S(2)}) async-start(), calls=%async_computation.2 | async-start | bytes 17825792 | tf_op jit(solution)/shard_map/all_gather | solution.py:47
  8.0 1215.1 %reduce-scatter.4.cloned.1.call-start = ((), (), s32[]{:S(2)}) async-start(), calls=%async_computation.3 | async-start | bytes 2359296
  237.8 15.5 %collective-permute-start = (bf16[128,2048]{1,0:T(8,128)(2,1)}, bf16[128,2048]{1,0:T(8,128)(2,1)}, u32[]{:S(2)}, u32[]{:S(2)}) collective-permute-start(bf16[128,2048]{1,0:T(8,128)(2,1)} %get-tuple-element.1314), channel_id=1, source_target_pairs={{16,0},{32,16},{48,32},{64,48},{80,64},{96,80},{112,96},{17,1},{33... | collective-permute-start | bytes 1572872 | tf_op jit(solution)/shard_map/while/body/eval_jaxpr/ppermute | solution.py:22
  255.2 14.6 %collective-permute-start = (bf16[128,2048]{1,0:T(8,128)(2,1)}, bf16[128,2048]{1,0:T(8,128)(2,1)}, u32[]{:S(2)}, u32[]{:S(2)}) collective-permute-start(bf16[128,2048]{1,0:T(8,128)(2,1)} %get-tuple-element.1314), channel_id=1, source_target_pairs={{16,0},{32,16},{48,32},{64,48},{80,64},{96,80},{112,96},{17,1},{33... | collective-permute-start | bytes 1572872 | tf_op jit(solution)/shard_map/while/body/eval_jaxpr/ppermute | solution.py:22
  271.7 14.6 %collective-permute-start = (bf16[128,2048]{1,0:T(8,128)(2,1)}, bf16[128,2048]{1,0:T(8,128)(2,1)}, u32[]{:S(2)}, u32[]{:S(2)}) collective-permute-start(bf16[128,2048]{1,0:T(8,128)(2,1)} %get-tuple-element.1314), channel_id=1, source_target_pairs={{16,0},{32,16},{48,32},{64,48},{80,64},{96,80},{112,96},{17,1},{33... | collective-permute-start | bytes 1572872 | tf_op jit(solution)/shard_map/while/body/eval_jaxpr/ppermute | solution.py:22
  288.2 13.6 %collective-permute-start = (bf16[128,2048]{1,0:T(8,128)(2,1)}, bf16[128,2048]{1,0:T(8,128)(2,1)}, u32[]{:S(2)}, u32[]{:S(2)}) collective-permute-start(bf16[128,2048]{1,0:T(8,128)(2,1)} %get-tuple-element.1314), channel_id=1, source_target_pairs={{16,0},{32,16},{48,32},{64,48},{80,64},{96,80},{112,96},{17,1},{33... | collective-permute-start | bytes 1572872 | tf_op jit(solution)/shard_map/while/body/eval_jaxpr/ppermute | solution.py:22
  303.7 12.7 %collective-permute-start = (bf16[128,2048]{1,0:T(8,128)(2,1)}, bf16[128,2048]{1,0:T(8,128)(2,1)}, u32[]{:S(2)}, u32[]{:S(2)}) collective-permute-start(bf16[128,2048]{1,0:T(8,128)(2,1)} %get-tuple-element.1314), channel_id=1, source_target_pairs={{16,0},{32,16},{48,32},{64,48},{80,64},{96,80},{112,96},{17,1},{33... | collective-permute-start | bytes 1572872 | tf_op jit(solution)/shard_map/while/body/eval_jaxpr/ppermute | solution.py:22
  318.3 11.8 collective-permute-start
  332.0 176.7 %collective-permute-start = (bf16[128,2048]{1,0:T(8,128)(2,1)}, bf16[128,2048]{1,0:T(8,128)(2,1)}, u32[]{:S(2)}, u32[]{:S(2)}) collective-permute-start(bf16[128,2048]{1,0:T(8,128)(2,1)} %get-tuple-element.1314), channel_id=1, source_target_pairs={{16,0},{32,16},{48,32},{64,48},{80,64},{96,80},{112,96},{17,1},{33... | collective-permute-start | bytes 1572872 | tf_op jit(solution)/shard_map/while/body/eval_jaxpr/ppermute | solution.py:22
  509.1 83.7 %collective-permute-start.2 = (bf16[4,128,2048]{2,1,0:T(8,128)(2,1)}, bf16[4,128,2048]{2,1,0:T(8,128)(2,1)S(1)}, u32[]{:S(2)}, u32[]{:S(2)}) collective-permute-start(bf16[4,128,2048]{2,1,0:T(8,128)(2,1)} %get-tuple-element.1061), channel_id=1, source_target_pairs={{0,16},{16,0},{32,48},{48,32},{64,80},{80,64},{96,112},{112,96},{1... | collective-permute-start | bytes 6291464 | tf_op jit(solution)/shard_map/ppermute | solution.py:16
  592.8 120.2 %collective-permute-start.3 = (bf16[4,128,2048]{2,1,0:T(8,128)(2,1)S(1)}, bf16[4,128,2048]{2,1,0:T(8,128)(2,1)}, u32[]{:S(2)}, u32[]{:S(2)}) collective-permute-start(bf16[4,128,2048]{2,1,0:T(8,128)(2,1)S(1)} %collective-permute-done.2), channel_id=1, source_target_pairs={{0,32},{16,48},{32,0},{48,16},{64,96},{80,112},{96,64},{112,80},{1... | collective-permute-start | bytes 6291464 | tf_op jit(solution)/shard_map/ppermute | solution.py:16
  713.0 47.9 %collective-permute-start.4 = (bf16[4,128,2048]{2,1,0:T(8,128)(2,1)}, bf16[4,128,2048]{2,1,0:T(8,128)(2,1)}, u32[]{:S(2)}, u32[]{:S(2)}) collective-permute-start(bf16[4,128,2048]{2,1,0:T(8,128)(2,1)} %collective-permute-done.3), channel_id=1, source_target_pairs={{0,64},{16,80},{32,96},{48,112},{64,0},{80,16},{96,32},{112,48},{1... | collective-permute-start | bytes 6291464 | tf_op jit(solution)/shard_map/ppermute | solution.py:16
  764.8 10.1 collective-permute-start.1
  780.1 11.6 collective-permute-start.1
  796.8 132.9 %collective-permute-start.1 = (bf16[128,2048]{1,0:T(8,128)(2,1)}, bf16[128,2048]{1,0:T(8,128)(2,1)S(1)}, u32[]{:S(2)}, u32[]{:S(2)}) collective-permute-start(bf16[128,2048]{1,0:T(8,128)(2,1)} %get-tuple-element.1335), channel_id=1, source_target_pairs={{16,0},{32,16},{48,32},{64,48},{80,64},{96,80},{112,96},{17,1},{33... | collective-permute-start | bytes 1572872 | tf_op jit(solution)/shard_map/while/body/eval_jaxpr/ppermute | solution.py:22
  958.2 3.7 copy-start.6
  976.0 11.0 collective-permute-start.1
  1015.6 3.7 copy-start.6
  1033.4 11.0 collective-permute-start.1
  1072.9 3.7 copy-start.6
  1090.7 11.0 collective-permute-start.1
  1148.1 10.1 collective-permute-start.1
  1159.4 65.3 %copy-start.1 = (f32[4,2048]{1,0:T(4,128)S(1)}, f32[4,2048]{1,0:T(4,128)}, u32[]{:S(2)}) copy-start(f32[4,2048]{1,0:T(4,128)} %param.19) | copy-start | bytes 98308
  (7 other events, 22.1 us)
Sparse Core Ops, SparseCore 0:
  9.8 113.8 all-gather.2
  126.1 107.9 all-gather.4
  1161.6 61.4 reduce-scatter.3
where the time goes:
time: 1230 us
  waiting for transfers between devices  834 us (68%)
  matrix products  162 us (13%)
  starting transfers between devices  148 us (12%)
  other arithmetic  36 us (3%)
  local copies, waits for them, and re-layouts  35.5 us (3%)
  between operations  13.2 us (1%)
    ppermute x14, waiting for transfers between devices, from_behind(): return lax.ppermute(value, axis, pairs)  424 us
    ppermute x3, starting transfers between devices, partner(): lax.ppermute(value, axis, [(i, i ^ 1 << bit) for i in range(lax.axis_size...  130 us
    ppermute x3, waiting for transfers between devices, partner(): lax.ppermute(value, axis, [(i, i ^ 1 << bit) for i in range(lax.axis_size...  121 us
    all_gather x1, waiting for transfers between devices, body(): lax.all_gather(w_out, 'shard', axis=1, tiled=True)  116 us
    all_gather x1, waiting for transfers between devices, body(): lax.all_gather(w_in, 'shard', axis=1, tiled=True)  110 us
    unnamed x4, waiting for transfers between devices  63 us
    dot_general x4, matrix products, compute(): lax.dot_general(grad, w_second, (((1,), (1,)), ((), ())), preferred_eleme...  52.4 us
    dot_general x4, matrix products, compute(): lax.dot_general(grad_pre, w_first, (((1,), (1,)), ((), ())), preferred_el...  50.3 us
  transfers between devices with their start and end apart: 20, of which 20 were waited for; matrix products, arithmetic and copies ran while one was open for 1% of the time, Pallas kernels for 0%

commit v1 on v0

v1 whole, which is shorter than its diff:
```python
import functools
import math

import jax
import jax.numpy as jnp
from jax import lax
from jax.experimental import pallas as pl
from jax.experimental.pallas import tpu as pltpu
from jax.sharding import PartitionSpec as P

MESH = pl.DeviceIdType.MESH
SEQ = 256
SECTIONS = 8
CHIPS = 8
PIECES = 4
CHUNKS = 4
square_root_half = 1.0 / math.sqrt(2.0)
inv_root_two_pi = 1.0 / math.sqrt(2.0 * math.pi)

POSITIONS = ("own", "xm", "xp", "x2a", "x2b", "yo", "pm", "pp", "p2a", "p2b")
ITEMS = (
    ("in", 0, 1792, False),
    ("in", 1792, 2304, True),
    ("out", 0, 896, False),
    ("out", 896, 1152, True),
)
EVENTS = {}
for _item in range(len(ITEMS)):
    for _pos in POSITIONS:
        if _pos != "own":
            EVENTS[(_item, _pos, "link")] = len(EVENTS)
        EVENTS[(_item, _pos, "core")] = len(EVENTS)


def forwards(pos, y_first):
    table = {
        "own": [("xm", "right"), ("xp", "left"), ("yo", "across")],
        "xm": [("x2a", "right")],
        "xp": [("x2b", "left")],
        "x2a": [],
        "x2b": [],
        "yo": [],
        "pm": [],
        "pp": [],
        "p2a": [],
        "p2b": [],
    }
    if y_first:
        table["yo"] = [("pm", "right"), ("pp", "left")]
        table["pm"] = [("p2a", "right")]
        table["pp"] = [("p2b", "left")]
    else:
        table["xm"] = table["xm"] + [("pm", "across")]
        table["xp"] = table["xp"] + [("pp", "across")]
        table["x2a"] = [("p2a", "across")]
        table["x2b"] = [("p2b", "across")]
    return table[pos]


def gelu_parts(value):
    cumulative = 0.5 * (1.0 + lax.erf(value * square_root_half))
    density = jnp.exp(-0.5 * value * value) * inv_root_two_pi
    return (value * cumulative, cumulative + value * density)


def nt(a, b):
    return lax.dot_general(a, b, (((1,), (1,)), ((), ())), preferred_element_type=jnp.float32)


def nn(a, b):
    return jnp.dot(a, b, preferred_element_type=jnp.float32)


def kernel(
    x_ref, g_ref, wi_ref, wo_ref, gain_ref, pm_ref, ph_ref, out_ref,
    wi, wo, xs, slope, inbox, skipbox, stage, gu, acc, in_a, in_b, term, parts,
    load_sem, ssem, rsem, swap_ssem, swap_rsem,
    next_ssem, next_rsem, skip_ssem, skip_rsem, last_ssem, last_rsem,
):
    s = lax.axis_index("section")
    h = lax.axis_index("shard")
    yh, x, c = h // 8, (h // 2) % 4, h % 2
    even = lax.rem(s, 2) == 0
    tokens, width = xs.shape
    hidden_width = slope.shape[1]
    piece = tokens // PIECES
    chunk = width // CHUNKS
    tile = 256

    def device(section, hi, xx, core):
        return (section, hi * 8 + xx * 2 + core)

    right = device(s, yh, (x + 1) % 4, c)
    left = device(s, yh, (x + 3) % 4, c)
    across = device(s, 1 - yh, x, c)
    sibling = device(s, yh, x, 1 - c)
    crossed = (yh + c) % 2
    below = device(jnp.maximum(s - 1, 0), crossed, x, c)
    mirror = device(SECTIONS - 1 - s, crossed, x, c)
    home_hi = jnp.where(even, crossed, yh)
    toward = {"right": right, "left": left, "across": across}

    barrier = pltpu.get_barrier_semaphore()
    for there in (right, left, sibling, across):
        pl.semaphore_signal(barrier, inc=1, device_id=there, device_id_type=MESH)
    for step in range(1, SECTIONS):
        for hi in range(2):
            pl.semaphore_signal(
                barrier, inc=1, device_id=device((s + step) % SECTIONS, hi, x, c), device_id_type=MESH
            )

    own_chip = yh * 4 + x
    load_in = pltpu.make_async_copy(
        wi_ref, wi.at[own_chip, :, pl.ds(pl.multiple_of(c * 128, 128), 128)], load_sem.at[0]
    )
    load_out = pltpu.make_async_copy(wo_ref, wo.at[h], load_sem.at[1])
    load_x = pltpu.make_async_copy(x_ref, xs, load_sem.at[2])
    load_g = pltpu.make_async_copy(g_ref, inbox, load_sem.at[3])
    load_in.start()
    load_out.start()
    swapped = even & (c == 1)

    @pl.when(jnp.logical_not(swapped))
    def _():
        load_x.start()

    @pl.when(s == SECTIONS - 1)
    def _():
        load_g.start()

    load_in.wait()
    load_out.wait()

    @pl.when(jnp.logical_not(swapped))
    def _():
        load_x.wait()

    @pl.when(s == SECTIONS - 1)
    def _():
        load_g.wait()

    pl.semaphore_wait(barrier, 4 + 2 * (SECTIONS - 1))

    def slab(item, pos, core):
        array, first, rows, _ = ITEMS[item]
        hi = yh if pos in ("own", "xm", "xp", "x2a", "x2b") else 1 - yh
        step = {"own": 0, "yo": 0, "xm": 3, "pm": 3, "xp": 1, "pp": 1}.get(pos, 2)
        half = pos[-1] if pos[-1] in "ab" else ""
        return slab_at(array, hi * 4 + (x + step) % 4, core, first, rows, half)

    def slab_at(array, chip, core, first, rows, half):
        if half:
            rows = rows // 2
            first = first + (rows if half == "b" else 0)
        if array == "in":
            return wi.at[chip, pl.ds(first, rows), pl.ds(pl.multiple_of(core * 128, 128), 128)]
        return wo.at[chip * 2 + core, pl.ds(first, rows), :]

    def copy_of(item, pos, kind, src, there):
        event = EVENTS[(item, pos, kind)]
        return pltpu.make_async_remote_copy(
            src_ref=src, dst_ref=src, send_sem=ssem.at[event], recv_sem=rsem.at[event],
            device_id=there, device_id_type=MESH,
        )

    def source(item, pos, there_pos):
        array, first, rows, _ = ITEMS[item]
        half = there_pos[-1] if there_pos[-1] in "ab" else ""
        hi = yh if pos in ("own", "xm", "xp", "x2a", "x2b") else 1 - yh
        step = {"own": 0, "yo": 0, "xm": 3, "pm": 3, "xp": 1, "pp": 1}.get(pos, 2)
        return slab_at(array, hi * 4 + (x + step) % 4, c, first, rows, half)

    sends = []

    def pass_on(item, pos):
        for there_pos, direction in forwards(pos, ITEMS[item][3]):
            cp = copy_of(item, there_pos, "link", source(item, pos, there_pos), toward[direction])
            cp.start()
            sends.append((item, pos, there_pos, direction))
        cp = copy_of(item, pos, "core", slab(item, pos, c), sibling)
        cp.start()
        sends.append((item, pos, pos, "core"))

    def receive(item, pos):
        copy_of(item, pos, "link", slab(item, pos, c), sibling).wait_recv()
        pass_on(item, pos)

    def receive_core(item, pos):
        copy_of(item, pos, "core", slab(item, pos, 1 - c), sibling).wait_recv()

    pass_on(0, "own")
    pass_on(1, "own")
    swap_x = pltpu.make_async_remote_copy(
        src_ref=x_ref, dst_ref=xs, send_sem=swap_ssem, recv_sem=swap_rsem, device_id=across, device_id_type=MESH
    )

    @pl.when(swapped)
    def _():
        swap_x.start()

    for item, pos in (
        (0, "xm"), (0, "xp"), (1, "yo"), (1, "xm"), (1, "xp"), (0, "yo"), (0, "x2a"), (0, "x2b"),
    ):
        receive(item, pos)
    pass_on(2, "own")
    pass_on(3, "own")
    for item, pos in (
        (1, "pm"), (1, "pp"), (0, "pm"), (0, "pp"), (1, "x2a"), (1, "x2b"),
        (2, "xm"), (2, "xp"),
        (0, "p2a"), (0, "p2b"), (1, "p2a"), (1, "p2b"),
    ):
        receive(item, pos)
    for item in (0, 1):
        for pos in POSITIONS:
            receive_core(item, pos)

    @pl.when(swapped)
    def _():
        swap_x.wait_recv()

    in_a[...] = nn(xs[...], pm_ref[...])
    in_b[...] = jnp.zeros_like(in_b)
    late = (
        (3, "yo"), (3, "xm"), (3, "xp"), (2, "yo"), (2, "x2a"), (2, "x2b"), (3, "pm"), (3, "pp"),
        (2, "pm"), (2, "pp"), (3, "x2a"), (3, "x2b"), (2, "p2a"), (2, "p2b"), (3, "p2a"), (3, "p2b"),
    )
    steps = hidden_width // tile

    @pl.loop(0, steps)
    def _(i):
        for at, (item, pos) in enumerate(late):
            @pl.when(i == at * steps // len(late))
            def _():
                receive(item, pos)

        cols = pl.ds(pl.multiple_of(i * tile, tile), tile)
        for part in range(tokens // 256):
            rows = pl.ds(part * 256, 256)
            u = nt(xs[rows, 0:tile], wi[0, cols, :])
            for chip in range(1, CHIPS):
                u = u + nt(xs[rows, chip * tile:(chip + 1) * tile], wi[chip, cols, :])
            act, slant = gelu_parts(u)
            slope[rows, cols] = slant
            in_b[rows, :] += nn(act.astype(jnp.bfloat16), ph_ref[cols, :])

    for item in (2, 3):
        for pos in POSITIONS:
            receive_core(item, pos)

    def chunk_copy(p, d, src, dst, send, recv, there):
        where = (pl.ds(pl.multiple_of(p * piece, piece), piece), pl.ds(d * chunk, chunk))
        return pltpu.make_async_remote_copy(
            src_ref=src.at[where], dst_ref=dst.at[where], send_sem=send.at[p, d], recv_sem=recv.at[p, d],
            device_id=there, device_id_type=MESH,
        )

    def to_next(p, d):
        return chunk_copy(p, d, stage, inbox, next_ssem, next_rsem, below)

    def to_skip(p, d):
        return chunk_copy(p, d, stage, skipbox, skip_ssem, skip_rsem, mirror)

    half = SECTIONS // 2
    gain_row = jnp.clip(half - 1 - s, 0, half - 1)

    @pl.loop(0, PIECES)
    def _(p):
        rows = pl.ds(pl.multiple_of(p * piece, piece), piece)
        for part in range(2):
            cols = pl.ds(part * (width // 2), width // 2)

            @pl.when(s < SECTIONS - 1)
            def _():
                for d in range(part * CHUNKS // 2, (part + 1) * CHUNKS // 2):
                    to_next(p, d).wait_recv()

            @pl.when(s < half - 1)
            def _():
                for d in range(part * CHUNKS // 2, (part + 1) * CHUNKS // 2):
                    to_skip(p, d).wait_recv()
                gain = gain_ref[pl.ds(gain_row, 1), cols]
                total = inbox[rows, cols].astype(jnp.float32) + gain * skipbox[rows, cols].astype(jnp.float32)
                inbox[rows, cols] = total.astype(jnp.bfloat16)

            @pl.when(s == half - 1)
            def _():
                gain = gain_ref[pl.ds(gain_row, 1), cols]
                value = inbox[rows, cols].astype(jnp.float32)
                inbox[rows, cols] = (value + gain * value).astype(jnp.bfloat16)

            @pl.loop(0, hidden_width // tile)
            def _(j):
                there = pl.ds(pl.multiple_of(j * tile, tile), tile)
                product = nn(inbox[rows, cols], wo[j, cols, :])
                if part == 0:
                    acc[:, there] = product
                else:
                    gu[rows, there] = ((acc[:, there] + product) * slope[rows, there]).astype(jnp.bfloat16)

        @pl.when(s > 0)
        def _():
            for d in range(CHUNKS):
                @pl.loop(0, chunk // tile)
                def _(k):
                    there = pl.ds(pl.multiple_of(d * chunk + k * tile, tile), tile)
                    grad_x = nn(gu[rows, :], wi[d * (chunk // tile) + k])
                    stage[rows, there] = (inbox[rows, there].astype(jnp.float32) + grad_x).astype(jnp.bfloat16)

                to_next(p, d).start()

                @pl.when(s > half)
                def _():
                    to_skip(p, d).start()

    for sample in range(tokens // SEQ):
        rows = pl.ds(sample * SEQ, SEQ)
        out_a = nn(gu[rows, :], ph_ref[...])
        out_b = nn(inbox[rows, :], pm_ref[...])

        def outer(a, b):
            return lax.dot_general(
                a, b, (((0,), (0,)), ((), ())), precision=lax.Precision.HIGHEST,
                preferred_element_type=jnp.float32,
            )

        first = outer(in_a[rows, :], out_a)
        second = pltpu.roll(outer(in_b[rows, :], out_b), 64, 1)
        term[sample] = (first[0:64, :] + second[64:128, :]) * (SEQ ** -0.5)

    def last_copy(t, index):
        return pltpu.make_async_remote_copy(
            src_ref=term.at[:, pl.ds(t * 8, 8), :], dst_ref=parts.at[index], send_sem=last_ssem.at[t],
            recv_sem=last_rsem.at[index], device_id=device(t, home_hi, x, c), device_id_type=MESH,
        )

    for t in range(SECTIONS):
        stays = (s == t) & jnp.logical_not(swapped)

        @pl.when(stays)
        def _():
            parts[t] = term[:, t * 8:(t + 1) * 8, :]

        @pl.when(jnp.logical_not(stays))
        def _():
            last_copy(t, s).start()

    for item, pos, there_pos, direction in sends:
        if direction == "core":
            copy_of(item, pos, "core", slab(item, pos, c), sibling).wait_send()
        else:
            copy_of(item, there_pos, "link", source(item, pos, there_pos), toward[direction]).wait_send()

    @pl.when(swapped)
    def _():
        swap_x.wait_send()

    @pl.loop(0, PIECES)
    def _(p):
        for d in range(CHUNKS):
            @pl.when(s > 0)
            def _():
                to_next(p, d).wait_send()

            @pl.when(s > half)
            def _():
                to_skip(p, d).wait_send()

    for t in range(SECTIONS):
        stays = (s == t) & jnp.logical_not(swapped)

        @pl.when(jnp.logical_not(stays))
        def _():
            last_copy(t, s).wait_send()
            last_copy(t, t).wait_recv()

    total = parts[0]
    for t in range(1, SECTIONS):
        total = total + parts[t]
    out_ref[...] = total


def body(saved_inputs, grad_out, w_in, w_out, skip_gain, proj_model, proj_hidden):
    tokens, width = grad_out.shape
    hidden_width = w_in.shape[2]
    samples = tokens // SEQ
    bf16, f32 = jnp.bfloat16, jnp.float32
    dma = pltpu.SemaphoreType.DMA
    result = pl.pallas_call(
        kernel,
        out_shape=jax.ShapeDtypeStruct((samples, 8, 128), f32),
        in_specs=[pl.BlockSpec(memory_space=pl.ANY)] * 4 + [pl.BlockSpec(memory_space=pltpu.VMEM)] * 3,
        out_specs=pl.BlockSpec(memory_space=pltpu.VMEM),
        scratch_shapes=[
            pltpu.VMEM((CHIPS, hidden_width, 256), bf16),
            pltpu.VMEM((2 * CHIPS, width, 256), bf16),
            pltpu.VMEM((tokens, width), bf16),
            pltpu.VMEM((tokens, hidden_width), f32),
            pltpu.VMEM((tokens, width), bf16),
            pltpu.VMEM((tokens, width), bf16),
            pltpu.VMEM((tokens, width), bf16),
            pltpu.VMEM((tokens, hidden_width), bf16),
            pltpu.VMEM((tokens // PIECES, hidden_width), f32),
            pltpu.VMEM((tokens, 128), f32),
            pltpu.VMEM((tokens, 128), f32),
            pltpu.VMEM((samples, 64, 128), f32),
            pltpu.VMEM((SECTIONS, samples, 8, 128), f32),
            dma((4,)),
            dma((len(EVENTS),)),
            dma((len(EVENTS),)),
            dma,
            dma,
            dma((PIECES, CHUNKS)),
            dma((PIECES, CHUNKS)),
            dma((PIECES, CHUNKS)),
            dma((PIECES, CHUNKS)),
            dma((SECTIONS,)),
            dma((SECTIONS,)),
        ],
        compiler_params=pltpu.CompilerParams(
            collective_id=0, has_side_effects=True, vmem_limit_bytes=62 * 2**20
        ),
    )(saved_inputs[0], grad_out, w_in[0].T, w_out[0].T, skip_gain, proj_model[0], proj_hidden[0])
    return result[:, :, :64].reshape(samples, 512)


def solution(mesh):
    placed = (
        P("section", "shard", None),
        P("shard", None),
        P("section", "shard", None),
        P("section", "shard", None),
        P(),
        P("section", None, None),
        P("section", None, None),
    )
    return jax.shard_map(
        body, mesh=mesh, in_specs=placed, out_specs=P("shard", "section"), check_vma=False
    )
```

time: 1230 us -> 302 us (0.25)
  waiting for transfers between devices: 834 us -> 0 us
  Pallas kernels: 0 us -> 292 us
  matrix products: 162 us -> 0 us
  starting transfers between devices: 148 us -> 0 us
  other arithmetic: 36 us -> 0 us
  local copies, waits for them, and re-layouts: 35.5 us -> 5.05 us
  between operations: 13.2 us -> 0.01 us
    ppermute x17 -> x0, waiting for transfers between devices: 545 us -> none  [the longest x14 424 us: from_behind(): return lax.ppermute(value, axis, pairs)]
    pallas_call x0 -> x1, Pallas kernels: none -> 292 us  [body(): pl.pallas_call(kernel, out_shape=jax.ShapeDtypeStruct((samples, 8, 128),...]
    all_gather x2 -> x0, waiting for transfers between devices: 226 us -> none  [the longest x1 116 us: body(): lax.all_gather(w_out, 'shard', axis=1, tiled=True)]
    dot_general x36 -> x0, matrix products: 162 us -> none  [the longest x4 52.4 us: compute(): lax.dot_general(grad, w_second, (((1,), (1,)), ((), ())), preferred_eleme...]
    ppermute x17 -> x0, starting transfers between devices: 148 us -> none  [the longest x3 130 us: partner(): lax.ppermute(value, axis, [(i, i ^ 1 << bit) for i in range(lax.axis_size...]
    unnamed x4 -> x0, waiting for transfers between devices: 63 us -> none
    dynamic_update_slice x35 -> x0, other arithmetic: 16.3 us -> none  [the longest x21 16.2 us: place(): lax.dynamic_update_index_in_dim(buffer, jnp.where(valid, value, old), slo...]
    dynamic_slice x15 -> x0, local copies, waits for them, and re-layouts: 15.2 us -> none  [the longest x14 15.1 us: place(): old = lax.dynamic_index_in_dim(buffer, slot, 0, keepdims=False)]
  transfers between devices with their start and end apart: 20 -> 0, of which waited for: 20 -> 0; matrix products, arithmetic and copies ran while one was open for 1% -> 0% of each run, Pallas kernels for 0% -> 0%
where the time goes in v1:
time: 302 us; the launch traced here: 298 us
  Pallas kernels  292 us (97%)
  local copies, waits for them, and re-layouts  5.05 us (2%)
    pallas_call x1, Pallas kernels, body(): pl.pallas_call(kernel, out_shape=jax.ShapeDtypeStruct((samples, 8, 128),...  292 us

profile of v1, /device:TPU:1, one launch (start us, length us, event | category | flops | bytes accessed | tf_op | source)
XLA Modules:
  0.0 297.5 jit_solution(9484176381649497517)
XLA Ops:
  0.0 0.0 copy-start
  0.0 2.4 copy.8
  2.4 0.0 copy-done
  2.4 1.3 copy.9
  3.7 292.4 %shard_map.73 = f32[2,8,128]{2,1,0:T(8,128)} custom-call(bf16[512,2048]{1,0:T(8,128)(2,1)} %bitcast.12, bf16[512,2048]{1,0:T(8,128)(2,1)} %g_ref.1, bf16[4096,128]{1,0:T(8,128)(2,1)} %bitcast.10, bf16[2048,256]{1,0:T(8,128)(2,1)} %bitcast.11, f32[4,2048]{1,0:T(4,128)} %gain_ref.1, bf16[2048,128]{1,0:T(8,128)(2,1)} %bitcast.14, bf16[4096,128]{1,0:T(8,128)(2,1)} %bitcast.13), custom_call_target="tpu_custom_call" | custom-call | tf_op jit(solution)/shard_map/pallas_call | solution.py:388
  296.1 1.4 reshape.3
Async XLA Ops:
  0.0 2.4 copy-start

commit v2 on v1

--- a/solution.py
+++ b/solution.py
@@ -14,6 +14,7 @@
 CHIPS = 8
 PIECES = 4
 CHUNKS = 4
+PARTS = 2
 square_root_half = 1.0 / math.sqrt(2.0)
 inv_root_two_pi = 1.0 / math.sqrt(2.0 * math.pi)
 
@@ -30,6 +31,19 @@
         if _pos != "own":
             EVENTS[(_item, _pos, "link")] = len(EVENTS)
         EVENTS[(_item, _pos, "core")] = len(EVENTS)
+
+
+EARLY = (
+    (0, "own"), (1, "own"),
+    (0, "xm"), (0, "xp"), (1, "yo"), (1, "xm"), (1, "xp"), (0, "yo"), (0, "x2a"), (0, "x2b"),
+    (2, "own"), (3, "own"), "swap",
+    (1, "pm"), (1, "pp"), (0, "pm"), (0, "pp"), (1, "x2a"), (1, "x2b"), (2, "xm"), (2, "xp"),
+    (0, "p2a"), (0, "p2b"), (1, "p2a"), (1, "p2b"),
+)
+LATE = (
+    (3, "yo"), (3, "xm"), (3, "xp"), (2, "yo"), (2, "x2a"), (2, "x2b"), (3, "pm"), (3, "pp"),
+    (2, "pm"), (2, "pp"), (3, "x2a"), (3, "x2b"), (2, "p2a"), (2, "p2b"), (3, "p2a"), (3, "p2b"),
+)
 
 
 def forwards(pos, y_first):
@@ -75,12 +89,15 @@
     x_ref, g_ref, wi_ref, wo_ref, gain_ref, pm_ref, ph_ref, out_ref,
     wi, wo, xs, slope, inbox, skipbox, stage, gu, acc, in_a, in_b, term, parts,
     load_sem, ssem, rsem, swap_ssem, swap_rsem,
-    next_ssem, next_rsem, skip_ssem, skip_rsem, last_ssem, last_rsem,
+    next_ssem, next_rsem, skip_ssem, skip_rsem, last_ssem, last_rsem, turn_sem,
 ):
     s = lax.axis_index("section")
     h = lax.axis_index("shard")
     yh, x, c = h // 8, (h // 2) % 4, h % 2
-    even = lax.rem(s, 2) == 0
+
+    def crosses(section):
+        return (lax.rem(section, 2) == 0) & (section < SECTIONS - 2)
+
     tokens, width = xs.shape
     hidden_width = slope.shape[1]
     piece = tokens // PIECES
@@ -94,10 +111,15 @@
     left = device(s, yh, (x + 3) % 4, c)
     across = device(s, 1 - yh, x, c)
     sibling = device(s, yh, x, 1 - c)
-    crossed = (yh + c) % 2
-    below = device(jnp.maximum(s - 1, 0), crossed, x, c)
-    mirror = device(SECTIONS - 1 - s, crossed, x, c)
-    home_hi = jnp.where(even, crossed, yh)
+    swapped = crosses(s) & (c == 1)
+
+    def facing(section):
+        cross = (crosses(s) | crosses(section)) & (c == 1)
+        return device(section, jnp.where(cross, 1 - yh, yh), x, c)
+
+    below = facing(jnp.maximum(s - 1, 0))
+    mirror = facing(SECTIONS - 1 - s)
+    home_hi = jnp.where(swapped, 1 - yh, yh)
     toward = {"right": right, "left": left, "across": across}
 
     barrier = pltpu.get_barrier_semaphore()
@@ -110,16 +132,13 @@
             )
 
     own_chip = yh * 4 + x
-    load_in = pltpu.make_async_copy(
-        wi_ref, wi.at[own_chip, :, pl.ds(pl.multiple_of(c * 128, 128), 128)], load_sem.at[0]
-    )
-    load_out = pltpu.make_async_copy(wo_ref, wo.at[h], load_sem.at[1])
-    load_x = pltpu.make_async_copy(x_ref, xs, load_sem.at[2])
+    slab_in, slab_out = wi_ref.shape[1], wo_ref.shape[1]
+    load_in = pltpu.make_async_copy(wi_ref.at[0], gu.at[pl.ds(0, slab_in)], load_sem.at[0])
+    load_out = pltpu.make_async_copy(wo_ref.at[0], stage.at[pl.ds(0, slab_out)], load_sem.at[1])
+    load_x = pltpu.make_async_copy(x_ref.at[0], xs, load_sem.at[2])
     load_g = pltpu.make_async_copy(g_ref, inbox, load_sem.at[3])
     load_in.start()
     load_out.start()
-    swapped = even & (c == 1)
-
     @pl.when(jnp.logical_not(swapped))
     def _():
         load_x.start()
@@ -129,7 +148,12 @@
         load_g.start()
 
     load_in.wait()
+    own_cols = pl.ds(pl.multiple_of(c * slab_in, slab_in), slab_in)
+    for first in range(0, hidden_width, 512):
+        wi[own_chip, first:first + 512, own_cols] = gu[0:slab_in, first:first + 512].T
     load_out.wait()
+    for first in range(0, width, 512):
+        wo[h, first:first + 512, :] = stage[0:slab_out, first:first + 512].T
 
     @pl.when(jnp.logical_not(swapped))
     def _():
@@ -188,28 +212,18 @@
     def receive_core(item, pos):
         copy_of(item, pos, "core", slab(item, pos, 1 - c), sibling).wait_recv()
 
-    pass_on(0, "own")
-    pass_on(1, "own")
     swap_x = pltpu.make_async_remote_copy(
-        src_ref=x_ref, dst_ref=xs, send_sem=swap_ssem, recv_sem=swap_rsem, device_id=across, device_id_type=MESH
+        src_ref=x_ref.at[0], dst_ref=xs, send_sem=swap_ssem, recv_sem=swap_rsem, device_id=across, device_id_type=MESH
     )
-
-    @pl.when(swapped)
-    def _():
-        swap_x.start()
-
-    for item, pos in (
-        (0, "xm"), (0, "xp"), (1, "yo"), (1, "xm"), (1, "xp"), (0, "yo"), (0, "x2a"), (0, "x2b"),
-    ):
-        receive(item, pos)
-    pass_on(2, "own")
-    pass_on(3, "own")
-    for item, pos in (
-        (1, "pm"), (1, "pp"), (0, "pm"), (0, "pp"), (1, "x2a"), (1, "x2b"),
-        (2, "xm"), (2, "xp"),
-        (0, "p2a"), (0, "p2b"), (1, "p2a"), (1, "p2b"),
-    ):
-        receive(item, pos)
+    for entry in EARLY:
+        if entry == "swap":
+            @pl.when(swapped)
+            def _():
+                swap_x.start()
+        elif entry[1] == "own":
+            pass_on(*entry)
+        else:
+            receive(*entry)
     for item in (0, 1):
         for pos in POSITIONS:
             receive_core(item, pos)
@@ -220,16 +234,12 @@
 
     in_a[...] = nn(xs[...], pm_ref[...])
     in_b[...] = jnp.zeros_like(in_b)
-    late = (
-        (3, "yo"), (3, "xm"), (3, "xp"), (2, "yo"), (2, "x2a"), (2, "x2b"), (3, "pm"), (3, "pp"),
-        (2, "pm"), (2, "pp"), (3, "x2a"), (3, "x2b"), (2, "p2a"), (2, "p2b"), (3, "p2a"), (3, "p2b"),
-    )
     steps = hidden_width // tile
 
     @pl.loop(0, steps)
     def _(i):
-        for at, (item, pos) in enumerate(late):
-            @pl.when(i == at * steps // len(late))
+        for at, (item, pos) in enumerate(LATE):
+            @pl.when(i == at * steps // len(LATE))
             def _():
                 receive(item, pos)
 
@@ -266,17 +276,18 @@
     @pl.loop(0, PIECES)
     def _(p):
         rows = pl.ds(pl.multiple_of(p * piece, piece), piece)
-        for part in range(2):
-            cols = pl.ds(part * (width // 2), width // 2)
+        for part in range(PARTS):
+            cols = pl.ds(part * (width // PARTS), width // PARTS)
+            chunks = range(part * CHUNKS // PARTS, (part + 1) * CHUNKS // PARTS)
 
             @pl.when(s < SECTIONS - 1)
             def _():
-                for d in range(part * CHUNKS // 2, (part + 1) * CHUNKS // 2):
+                for d in chunks:
                     to_next(p, d).wait_recv()
 
             @pl.when(s < half - 1)
             def _():
-                for d in range(part * CHUNKS // 2, (part + 1) * CHUNKS // 2):
+                for d in chunks:
                     to_skip(p, d).wait_recv()
                 gain = gain_ref[pl.ds(gain_row, 1), cols]
                 total = inbox[rows, cols].astype(jnp.float32) + gain * skipbox[rows, cols].astype(jnp.float32)
@@ -288,14 +299,24 @@
                 value = inbox[rows, cols].astype(jnp.float32)
                 inbox[rows, cols] = (value + gain * value).astype(jnp.bfloat16)
 
-            @pl.loop(0, hidden_width // tile)
-            def _(j):
-                there = pl.ds(pl.multiple_of(j * tile, tile), tile)
-                product = nn(inbox[rows, cols], wo[j, cols, :])
-                if part == 0:
-                    acc[:, there] = product
-                else:
-                    gu[rows, there] = ((acc[:, there] + product) * slope[rows, there]).astype(jnp.bfloat16)
+            @pl.loop(0, hidden_width // (4 * tile))
+            def _(group):
+                for one in range(4):
+                    j = group * 4 + one
+                    there = pl.ds(pl.multiple_of(j * tile, tile), tile)
+                    product = nn(inbox[rows, cols], wo[j, cols, :])
+                    if part == 0:
+                        acc[:, there] = product
+                    elif part < PARTS - 1:
+                        acc[:, there] += product
+                    else:
+                        gu[rows, there] = ((acc[:, there] + product) * slope[rows, there]).astype(jnp.bfloat16)
+
+        first_turn = (s == SECTIONS - 1) & (p == 0)
+
+        @pl.when(first_turn & (c == 1))
+        def _():
+            pl.semaphore_wait(turn_sem, 1)
 
         @pl.when(s > 0)
         def _():
@@ -308,9 +329,16 @@
 
                 to_next(p, d).start()
 
-                @pl.when(s > half)
-                def _():
-                    to_skip(p, d).start()
+        for q in range(PIECES):
+            soon = (s == half + 1) & (p == min(q + 1, PIECES - 1))
+            @pl.when(soon | ((s > half + 1) & (p == PIECES - 1)))
+            def _():
+                for d in range(CHUNKS):
+                    to_skip(q, d).start()
+
+        @pl.when(first_turn & (c == 0))
+        def _():
+            pl.semaphore_signal(turn_sem, inc=1, device_id=sibling, device_id_type=MESH)
 
     for sample in range(tokens // SEQ):
         rows = pl.ds(sample * SEQ, SEQ)
@@ -415,11 +443,12 @@
             dma((PIECES, CHUNKS)),
             dma((SECTIONS,)),
             dma((SECTIONS,)),
+            pltpu.SemaphoreType.REGULAR,
         ],
         compiler_params=pltpu.CompilerParams(
             collective_id=0, has_side_effects=True, vmem_limit_bytes=62 * 2**20
         ),
-    )(saved_inputs[0], grad_out, w_in[0].T, w_out[0].T, skip_gain, proj_model[0], proj_hidden[0])
+    )(saved_inputs, grad_out, w_in, w_out, skip_gain, proj_model[0], proj_hidden[0])
     return result[:, :, :64].reshape(samples, 512)
 
 

time: 302 us -> 259 us (0.86); the launches traced: 298 us -> 259 us
  Pallas kernels: 292 us -> 257 us
  local copies, waits for them, and re-layouts: 5.05 us -> 1.37 us
    pallas_call x1, Pallas kernels: 292 us -> 257 us  [body(): pl.pallas_call(kernel, out_shape=jax.ShapeDtypeStruct((samples, 8, 128),...]
    unnamed x4 -> x0, local copies, waits for them, and re-layouts: 3.69 us -> none
where the time goes in v2:
time: 259 us
  Pallas kernels  257 us (99%)
    pallas_call x1, Pallas kernels, body(): pl.pallas_call(kernel, out_shape=jax.ShapeDtypeStruct((samples, 8, 128),...  257 us

profile of v2, /device:TPU:1, one launch (start us, length us, event | category | flops | bytes accessed | tf_op | source)
XLA Modules:
  0.0 258.8 jit_solution(6327500507547555290)
XLA Ops:
  0.0 257.5 %shard_map.73 = f32[2,8,128]{2,1,0:T(8,128)} custom-call(bf16[1,512,2048]{2,1,0:T(8,128)(2,1)} %x_ref.1, bf16[512,2048]{1,0:T(8,128)(2,1)} %g_ref.1, bf16[1,128,4096]{2,1,0:T(8,128)(2,1)} %wi_ref.1, bf16[1,256,2048]{2,1,0:T(8,128)(2,1)} %wo_ref.1, f32[4,2048]{1,0:T(4,128)} %gain_ref.1, bf16[2048,128]{1,0:T(8,128)(2,1)} %bitcast.4, bf16[4096,128]{1,0:T(8,128)(2,1)} %bitcast.3), custom_call_target="tpu_custom_call" | custom-call | tf_op jit(solution)/shard_map/pallas_call | solution.py:416
  257.5 1.4 reshape.3

commit v3 on v2

--- a/solution.py
+++ b/solution.py
@@ -34,7 +34,7 @@
 
 
 EARLY = (
-    (0, "own"), (1, "own"),
+    (0, "own"), (1, "own"), "rest",
     (0, "xm"), (0, "xp"), (1, "yo"), (1, "xm"), (1, "xp"), (0, "yo"), (0, "x2a"), (0, "x2b"),
     (2, "own"), (3, "own"), "swap",
     (1, "pm"), (1, "pp"), (0, "pm"), (0, "pp"), (1, "x2a"), (1, "x2b"), (2, "xm"), (2, "xp"),
@@ -44,6 +44,7 @@
     (3, "yo"), (3, "xm"), (3, "xp"), (2, "yo"), (2, "x2a"), (2, "x2b"), (3, "pm"), (3, "pp"),
     (2, "pm"), (2, "pp"), (3, "x2a"), (3, "x2b"), (2, "p2a"), (2, "p2b"), (3, "p2a"), (3, "p2b"),
 )
+LAST = 4
 
 
 def forwards(pos, y_first):
@@ -86,10 +87,10 @@
 
 
 def kernel(
-    x_ref, g_ref, wi_ref, wo_ref, gain_ref, pm_ref, ph_ref, out_ref,
+    x_ref, g_ref, wi_ref, wo_ref, gain_ref, pm_hbm, ph_hbm, out_ref,
     wi, wo, xs, slope, inbox, skipbox, stage, gu, acc, in_a, in_b, term, parts,
     load_sem, ssem, rsem, swap_ssem, swap_rsem,
-    next_ssem, next_rsem, skip_ssem, skip_rsem, last_ssem, last_rsem, turn_sem,
+    next_ssem, next_rsem, skip_ssem, skip_rsem, last_ssem, last_rsem, turn_sem, pm_ref, ph_ref,
 ):
     s = lax.axis_index("section")
     h = lax.axis_index("shard")
@@ -101,6 +102,7 @@
     tokens, width = xs.shape
     hidden_width = slope.shape[1]
     piece = tokens // PIECES
+    samples = tokens // SEQ
     chunk = width // CHUNKS
     tile = 256
 
@@ -137,8 +139,12 @@
     load_out = pltpu.make_async_copy(wo_ref.at[0], stage.at[pl.ds(0, slab_out)], load_sem.at[1])
     load_x = pltpu.make_async_copy(x_ref.at[0], xs, load_sem.at[2])
     load_g = pltpu.make_async_copy(g_ref, inbox, load_sem.at[3])
+    load_pm = pltpu.make_async_copy(pm_hbm.at[0], pm_ref, load_sem.at[4])
+    load_ph = pltpu.make_async_copy(ph_hbm.at[0], ph_ref, load_sem.at[5])
     load_in.start()
     load_out.start()
+    load_pm.start()
+    load_ph.start()
     @pl.when(jnp.logical_not(swapped))
     def _():
         load_x.start()
@@ -151,18 +157,6 @@
     own_cols = pl.ds(pl.multiple_of(c * slab_in, slab_in), slab_in)
     for first in range(0, hidden_width, 512):
         wi[own_chip, first:first + 512, own_cols] = gu[0:slab_in, first:first + 512].T
-    load_out.wait()
-    for first in range(0, width, 512):
-        wo[h, first:first + 512, :] = stage[0:slab_out, first:first + 512].T
-
-    @pl.when(jnp.logical_not(swapped))
-    def _():
-        load_x.wait()
-
-    @pl.when(s == SECTIONS - 1)
-    def _():
-        load_g.wait()
-
     pl.semaphore_wait(barrier, 4 + 2 * (SECTIONS - 1))
 
     def slab(item, pos, core):
@@ -220,6 +214,10 @@
             @pl.when(swapped)
             def _():
                 swap_x.start()
+        elif entry == "rest":
+            load_out.wait()
+            for first in range(0, width, 512):
+                wo[h, first:first + 512, :] = stage[0:slab_out, first:first + 512].T
         elif entry[1] == "own":
             pass_on(*entry)
         else:
@@ -232,14 +230,25 @@
     def _():
         swap_x.wait_recv()
 
+    @pl.when(jnp.logical_not(swapped))
+    def _():
+        load_x.wait()
+
+    @pl.when(s == SECTIONS - 1)
+    def _():
+        load_g.wait()
+
+    load_pm.wait()
+    load_ph.wait()
+
     in_a[...] = nn(xs[...], pm_ref[...])
     in_b[...] = jnp.zeros_like(in_b)
     steps = hidden_width // tile
 
     @pl.loop(0, steps)
     def _(i):
-        for at, (item, pos) in enumerate(LATE):
-            @pl.when(i == at * steps // len(LATE))
+        for at, (item, pos) in enumerate(LATE[:-LAST]):
+            @pl.when(i == at * steps // len(LATE[:-LAST]))
             def _():
                 receive(item, pos)
 
@@ -253,6 +262,8 @@
             slope[rows, cols] = slant
             in_b[rows, :] += nn(act.astype(jnp.bfloat16), ph_ref[cols, :])
 
+    for item, pos in LATE[-LAST:]:
+        receive(item, pos)
     for item in (2, 3):
         for pos in POSITIONS:
             receive_core(item, pos)
@@ -269,6 +280,37 @@
 
     def to_skip(p, d):
         return chunk_copy(p, d, stage, skipbox, skip_ssem, skip_rsem, mirror)
+
+    def outer(a, b):
+        return lax.dot_general(
+            a, b, (((0,), (0,)), ((), ())), precision=lax.Precision.HIGHEST,
+            preferred_element_type=jnp.float32,
+        )
+
+    def last_copy(t, sample, index):
+        return pltpu.make_async_remote_copy(
+            src_ref=term.at[sample, pl.ds(t * 8, 8), :], dst_ref=parts.at[index, sample],
+            send_sem=last_ssem.at[t, sample], recv_sem=last_rsem.at[index, sample],
+            device_id=device(t, home_hi, x, c), device_id_type=MESH,
+        )
+
+    def finish(sample):
+        rows = pl.ds(sample * SEQ, SEQ)
+        out_a = nn(gu[rows, :], ph_ref[...])
+        out_b = nn(inbox[rows, :], pm_ref[...])
+        first = outer(in_a[rows, :], out_a)
+        second = pltpu.roll(outer(in_b[rows, :], out_b), 64, 1)
+        term[sample] = (first[0:64, :] + second[64:128, :]) * (SEQ ** -0.5)
+        for t in range(SECTIONS):
+            stays = (s == t) & jnp.logical_not(swapped)
+
+            @pl.when(stays)
+            def _():
+                parts[t, sample] = term[sample, t * 8:(t + 1) * 8, :]
+
+            @pl.when(jnp.logical_not(stays))
+            def _():
+                last_copy(t, sample, s).start()
 
     half = SECTIONS // 2
     gain_row = jnp.clip(half - 1 - s, 0, half - 1)
@@ -336,41 +378,16 @@
                 for d in range(CHUNKS):
                     to_skip(q, d).start()
 
+        for sample in range(samples - 1):
+            @pl.when(p == (sample + 1) * SEQ // piece - 1)
+            def _():
+                finish(sample)
+
         @pl.when(first_turn & (c == 0))
         def _():
             pl.semaphore_signal(turn_sem, inc=1, device_id=sibling, device_id_type=MESH)
 
-    for sample in range(tokens // SEQ):
-        rows = pl.ds(sample * SEQ, SEQ)
-        out_a = nn(gu[rows, :], ph_ref[...])
-        out_b = nn(inbox[rows, :], pm_ref[...])
-
-        def outer(a, b):
-            return lax.dot_general(
-                a, b, (((0,), (0,)), ((), ())), precision=lax.Precision.HIGHEST,
-                preferred_element_type=jnp.float32,
-            )
-
-        first = outer(in_a[rows, :], out_a)
-        second = pltpu.roll(outer(in_b[rows, :], out_b), 64, 1)
-        term[sample] = (first[0:64, :] + second[64:128, :]) * (SEQ ** -0.5)
-
-    def last_copy(t, index):
-        return pltpu.make_async_remote_copy(
-            src_ref=term.at[:, pl.ds(t * 8, 8), :], dst_ref=parts.at[index], send_sem=last_ssem.at[t],
-            recv_sem=last_rsem.at[index], device_id=device(t, home_hi, x, c), device_id_type=MESH,
-        )
-
-    for t in range(SECTIONS):
-        stays = (s == t) & jnp.logical_not(swapped)
-
-        @pl.when(stays)
-        def _():
-            parts[t] = term[:, t * 8:(t + 1) * 8, :]
-
-        @pl.when(jnp.logical_not(stays))
-        def _():
-            last_copy(t, s).start()
+    finish(samples - 1)
 
     for item, pos, there_pos, direction in sends:
         if direction == "core":
@@ -398,8 +415,9 @@
 
         @pl.when(jnp.logical_not(stays))
         def _():
-            last_copy(t, s).wait_send()
-            last_copy(t, t).wait_recv()
+            for sample in range(samples):
+                last_copy(t, sample, s).wait_send()
+                last_copy(t, sample, t).wait_recv()
 
     total = parts[0]
     for t in range(1, SECTIONS):
@@ -416,7 +434,7 @@
     result = pl.pallas_call(
         kernel,
         out_shape=jax.ShapeDtypeStruct((samples, 8, 128), f32),
-        in_specs=[pl.BlockSpec(memory_space=pl.ANY)] * 4 + [pl.BlockSpec(memory_space=pltpu.VMEM)] * 3,
+        in_specs=[pl.BlockSpec(memory_space=pl.ANY)] * 4 + [pl.BlockSpec(memory_space=pltpu.VMEM)] + [pl.BlockSpec(memory_space=pl.ANY)] * 2,
         out_specs=pl.BlockSpec(memory_space=pltpu.VMEM),
         scratch_shapes=[
             pltpu.VMEM((CHIPS, hidden_width, 256), bf16),
@@ -432,7 +450,7 @@
             pltpu.VMEM((tokens, 128), f32),
             pltpu.VMEM((samples, 64, 128), f32),
             pltpu.VMEM((SECTIONS, samples, 8, 128), f32),
-            dma((4,)),
+            dma((6,)),
             dma((len(EVENTS),)),
             dma((len(EVENTS),)),
             dma,
@@ -441,14 +459,16 @@
             dma((PIECES, CHUNKS)),
             dma((PIECES, CHUNKS)),
             dma((PIECES, CHUNKS)),
-            dma((SECTIONS,)),
-            dma((SECTIONS,)),
+            dma((SECTIONS, samples)),
+            dma((SECTIONS, samples)),
             pltpu.SemaphoreType.REGULAR,
+            pltpu.VMEM(proj_model.shape[1:], bf16),
+            pltpu.VMEM(proj_hidden.shape[1:], bf16),
         ],
         compiler_params=pltpu.CompilerParams(
             collective_id=0, has_side_effects=True, vmem_limit_bytes=62 * 2**20
         ),
-    )(saved_inputs, grad_out, w_in, w_out, skip_gain, proj_model[0], proj_hidden[0])
+    )(saved_inputs, grad_out, w_in, w_out, skip_gain, proj_model, proj_hidden)
     return result[:, :, :64].reshape(samples, 512)
 
 

time: 259 us -> 256 us (0.988)
  Pallas kernels: 257 us -> 254 us
    pallas_call x1, Pallas kernels: 257 us -> 254 us  [body(): pl.pallas_call(kernel, out_shape=jax.ShapeDtypeStruct((samples, 8, 128),...]
where the time goes in v3:
time: 256 us
  Pallas kernels  254 us (99%)
    pallas_call x1, Pallas kernels, body(): pl.pallas_call(kernel, out_shape=jax.ShapeDtypeStruct((samples, 8, 128),...  254 us

profile of v3, /device:TPU:1, one launch (start us, length us, event | category | flops | bytes accessed | tf_op | source)
XLA Modules:
  0.0 255.6 jit_solution(3404102468308588536)
XLA Ops:
  0.0 254.2 %shard_map.73 = f32[2,8,128]{2,1,0:T(8,128)} custom-call(bf16[1,512,2048]{2,1,0:T(8,128)(2,1)} %x_ref.1, bf16[512,2048]{1,0:T(8,128)(2,1)} %g_ref.1, bf16[1,128,4096]{2,1,0:T(8,128)(2,1)} %wi_ref.1, bf16[1,256,2048]{2,1,0:T(8,128)(2,1)} %wo_ref.1, f32[4,2048]{1,0:T(4,128)} %gain_ref.1, bf16[1,2048,128]{2,1,0:T(8,128)(2,1)} %pm_hbm.1, ...), custom_call_target="tpu_custom_call" | custom-call | tf_op jit(solution)/shard_map/pallas_call | solution.py:434
  254.3 1.4 reshape.3

commit v4 on v3

--- a/solution.py
+++ b/solution.py
@@ -20,10 +20,10 @@
 
 POSITIONS = ("own", "xm", "xp", "x2a", "x2b", "yo", "pm", "pp", "p2a", "p2b")
 ITEMS = (
-    ("in", 0, 1792, False),
-    ("in", 1792, 2304, True),
-    ("out", 0, 896, False),
-    ("out", 896, 1152, True),
+    ("in", 0, 1856, False),
+    ("in", 1856, 2240, True),
+    ("out", 0, 928, False),
+    ("out", 928, 1120, True),
 )
 EVENTS = {}
 for _item in range(len(ITEMS)):

time: 256 us -> 255 us (level)
  no operation moved by 1% of the time
where the time goes in v4:
time: 255 us
  Pallas kernels  253 us (99%)
    pallas_call x1, Pallas kernels, body(): pl.pallas_call(kernel, out_shape=jax.ShapeDtypeStruct((samples, 8, 128),...  253 us

profile of v4, /device:TPU:1, one launch (start us, length us, event | category | flops | bytes accessed | tf_op | source)
XLA Modules:
  0.0 254.6 jit_solution(2685107953510520816)
XLA Ops:
  0.0 253.2 %shard_map.73 = f32[2,8,128]{2,1,0:T(8,128)} custom-call(bf16[1,512,2048]{2,1,0:T(8,128)(2,1)} %x_ref.1, bf16[512,2048]{1,0:T(8,128)(2,1)} %g_ref.1, bf16[1,128,4096]{2,1,0:T(8,128)(2,1)} %wi_ref.1, bf16[1,256,2048]{2,1,0:T(8,128)(2,1)} %wo_ref.1, f32[4,2048]{1,0:T(4,128)} %gain_ref.1, bf16[1,2048,128]{2,1,0:T(8,128)(2,1)} %pm_hbm.1, ...), custom_call_target="tpu_custom_call" | custom-call | tf_op jit(solution)/shard_map/pallas_call | solution.py:434
  253.2 1.4 reshape.3

commit v5 on v4

--- a/solution.py
+++ b/solution.py
@@ -20,10 +20,10 @@
 
 POSITIONS = ("own", "xm", "xp", "x2a", "x2b", "yo", "pm", "pp", "p2a", "p2b")
 ITEMS = (
-    ("in", 0, 1856, False),
-    ("in", 1856, 2240, True),
-    ("out", 0, 928, False),
-    ("out", 928, 1120, True),
+    ("in", 0, 1920, False),
+    ("in", 1920, 2176, True),
+    ("out", 0, 960, False),
+    ("out", 960, 1088, True),
 )
 EVENTS = {}
 for _item in range(len(ITEMS)):
@@ -379,13 +379,18 @@
                     to_skip(q, d).start()
 
         for sample in range(samples - 1):
-            @pl.when(p == (sample + 1) * SEQ // piece - 1)
+            @pl.when((s == 0) & (p == (sample + 1) * SEQ // piece - 1))
             def _():
                 finish(sample)
 
         @pl.when(first_turn & (c == 0))
         def _():
             pl.semaphore_signal(turn_sem, inc=1, device_id=sibling, device_id_type=MESH)
+
+    @pl.when(s > 0)
+    def _():
+        for sample in range(samples - 1):
+            finish(sample)
 
     finish(samples - 1)
 

time: 255 us -> 254 us (level)
  no operation moved by 1% of the time
where the time goes in v5:
time: 254 us
  Pallas kernels  253 us (100%)
    pallas_call x1, Pallas kernels, body(): pl.pallas_call(kernel, out_shape=jax.ShapeDtypeStruct((samples, 8, 128),...  253 us

profile of v5, /device:TPU:1, one launch (start us, length us, event | category | flops | bytes accessed | tf_op | source)
XLA Modules:
  0.0 254.3 jit_solution(6763823168640658517)
XLA Ops:
  0.0 252.9 %shard_map.73 = f32[2,8,128]{2,1,0:T(8,128)} custom-call(bf16[1,512,2048]{2,1,0:T(8,128)(2,1)} %x_ref.1, bf16[512,2048]{1,0:T(8,128)(2,1)} %g_ref.1, bf16[1,128,4096]{2,1,0:T(8,128)(2,1)} %wi_ref.1, bf16[1,256,2048]{2,1,0:T(8,128)(2,1)} %wo_ref.1, f32[4,2048]{1,0:T(4,128)} %gain_ref.1, bf16[1,2048,128]{2,1,0:T(8,128)(2,1)} %pm_hbm.1, ...), custom_call_target="tpu_custom_call" | custom-call | tf_op jit(solution)/shard_map/pallas_call | solution.py:439
  252.9 1.4 reshape.3

commit v6 on v5

--- a/solution.py
+++ b/solution.py
@@ -315,6 +315,17 @@
     half = SECTIONS // 2
     gain_row = jnp.clip(half - 1 - s, 0, half - 1)
 
+    def gather_sent():
+        for item, pos, there_pos, direction in sends:
+            if direction == "core":
+                copy_of(item, pos, "core", slab(item, pos, c), sibling).wait_send()
+            else:
+                copy_of(item, there_pos, "link", source(item, pos, there_pos), toward[direction]).wait_send()
+
+    @pl.when(s < half)
+    def _():
+        gather_sent()
+
     @pl.loop(0, PIECES)
     def _(p):
         rows = pl.ds(pl.multiple_of(p * piece, piece), piece)
@@ -341,10 +352,10 @@
                 value = inbox[rows, cols].astype(jnp.float32)
                 inbox[rows, cols] = (value + gain * value).astype(jnp.bfloat16)
 
-            @pl.loop(0, hidden_width // (4 * tile))
+            @pl.loop(0, hidden_width // (8 * tile))
             def _(group):
-                for one in range(4):
-                    j = group * 4 + one
+                for one in range(8):
+                    j = group * 8 + one
                     there = pl.ds(pl.multiple_of(j * tile, tile), tile)
                     product = nn(inbox[rows, cols], wo[j, cols, :])
                     if part == 0:
@@ -394,11 +405,9 @@
 
     finish(samples - 1)
 
-    for item, pos, there_pos, direction in sends:
-        if direction == "core":
-            copy_of(item, pos, "core", slab(item, pos, c), sibling).wait_send()
-        else:
-            copy_of(item, there_pos, "link", source(item, pos, there_pos), toward[direction]).wait_send()
+    @pl.when(s >= half)
+    def _():
+        gather_sent()
 
     @pl.when(swapped)
     def _():

time: 254 us -> 252 us (level)
  no operation moved by 1% of the time
where the time goes in v6:
time: 252 us
  Pallas kernels  251 us (100%)
    pallas_call x1, Pallas kernels, body(): pl.pallas_call(kernel, out_shape=jax.ShapeDtypeStruct((samples, 8, 128),...  251 us

profile of v6, /device:TPU:1, one launch (start us, length us, event | category | flops | bytes accessed | tf_op | source)
XLA Modules:
  0.0 252.0 jit_solution(2948611645083132819)
XLA Ops:
  0.0 250.6 %shard_map.73 = f32[2,8,128]{2,1,0:T(8,128)} custom-call(bf16[1,512,2048]{2,1,0:T(8,128)(2,1)} %x_ref.1, bf16[512,2048]{1,0:T(8,128)(2,1)} %g_ref.1, bf16[1,128,4096]{2,1,0:T(8,128)(2,1)} %wi_ref.1, bf16[1,256,2048]{2,1,0:T(8,128)(2,1)} %wo_ref.1, f32[4,2048]{1,0:T(4,128)} %gain_ref.1, bf16[1,2048,128]{2,1,0:T(8,128)(2,1)} %pm_hbm.1, ...), custom_call_target="tpu_custom_call" | custom-call | tf_op jit(solution)/shard_map/pallas_call | solution.py:448
  250.6 1.4 reshape.3
